TPU v7x, 32 devices: a whole 2x2x4 slice. The times are simulated.
32 devices in a mesh: dp: 8 (over z, y), rows: 4 (over x, core).
Axes of the slice: x: 2, y: 2, z: 4, core: 2. Of those that a mesh axis runs over, the one named last changes fastest.
Arguments:
- candidates: bfloat16 [16, 4, 32, 32, 1024], P('dp', None, 'rows'), may hold values from -40 to 40
- winners: int32 [16], P('dp'), may hold values from 0 to 3
- conv_weight: bfloat16 [9216, 512], P('dp'), may hold values from -0.0625 to 0.0625
- conv_bias: float32 [512], replicated, may hold values from -3 to 3
- gamma: float32 [1024], replicated, may hold values from 0.5 to 1.5
- beta: float32 [1024], replicated, may hold values from -3 to 3
- cotangent: bfloat16 [16, 32, 32, 512], P('dp', 'rows'), may hold values from -6 to 6
Outputs:
- output: bfloat16 [16, 32, 32, 512], P('dp', 'rows')
- grad_weight: float32 [9216, 512], P('dp')
- grad_bias: float32 [512], replicated
- grad_gamma: float32 [1024], replicated
- grad_beta: float32 [1024], replicated
All inputs are finite; a program needn't handle non-finite values.
Results may differ from a plain program's by a relative error of at most 0.003.
Values may be sent and summed in bfloat16 or wider, within the bound.
A program may use at most 128 MiB of HBM per device.

v0:
```python
import jax
import jax.numpy as jnp
from jax import lax
from jax.sharding import PartitionSpec as P

GROUPS = 32


EPSILON = 1e-05


def with_halo(cells, sides, width):
    for axis, dim in sides:
        count = lax.axis_size(axis)
        ends = count - 1
        head = lax.slice_in_dim(cells, 0, width, axis=dim)
        tail = lax.slice_in_dim(cells, cells.shape[dim] - width, cells.shape[dim], axis=dim)
        cells = jnp.concatenate(
            [
                lax.ppermute(tail, axis, [(i, (i + 1) % count) for i in range(ends)]),
                cells,
                lax.ppermute(head, axis, [((i + 1) % count, i) for i in range(ends)]),
            ],
            axis=dim,
        )
    return cells


def body(candidates, winners, conv_weight, conv_bias, gamma, beta, cotangent):
    images, cand_count, rows_here, width, channels = candidates.shape
    out_channels = conv_weight.shape[1]
    groups = GROUPS
    cell_count = images * rows_here * width
    picked = candidates[:, 0]
    for cand_index in range(1, cand_count):
        picked = jnp.where(
            (winners == cand_index)[:, None, None, None], candidates[:, cand_index], picked
        )
    grouped = picked.astype(jnp.float32).reshape(
        images, rows_here, width, groups, channels // groups
    )
    local_sums = (jnp.sum(grouped, axis=(1, 2, 4)), jnp.sum(grouped * grouped, axis=(1, 2, 4)))
    totals, squares = lax.psum((local_sums[0], local_sums[1]), "rows")
    total_count = rows_here * lax.axis_size("rows") * width * (channels // groups)
    group_mean = totals / total_count
    group_var = squares / total_count - group_mean * group_mean
    inverse = lax.rsqrt(group_var + EPSILON)
    normed = (
        (grouped - group_mean[:, None, None, :, None]) * inverse[:, None, None, :, None]
    ).reshape(images, rows_here, width, channels)
    preact = normed * gamma + beta
    activated = jax.nn.silu(preact).astype(jnp.bfloat16)
    full_weight = lax.all_gather(conv_weight, "dp", axis=0, tiled=True)
    padded = with_halo(activated, (("rows", 1),), 1)
    padded = jnp.pad(padded, ((0, 0), (0, 0), (1, 1), (0, 0)))
    patches = jnp.concatenate(
        [
            padded[
                :, 1 + shift_row : 1 + shift_row + rows_here, 1 + shift_col : 1 + shift_col + width
            ].reshape(cell_count, channels)
            for shift_row in (-1, 0, 1)
            for shift_col in (-1, 0, 1)
        ],
        axis=1,
    )
    conv_sum = jnp.dot(patches, full_weight, preferred_element_type=jnp.float32) + conv_bias
    residual = picked[..., :out_channels].reshape(cell_count, out_channels).astype(jnp.float32)
    output = (
        (conv_sum + residual).astype(jnp.bfloat16).reshape(images, rows_here, width, out_channels)
    )
    grad_scale = float(
        images * lax.axis_size("dp") * rows_here * lax.axis_size("rows") * width
    ) ** (-0.5)
    flat_cot = cotangent.reshape(cell_count, out_channels)
    bias_term = jnp.sum(flat_cot.astype(jnp.float32), axis=0) * grad_scale
    product = lax.dot_general(
        patches, flat_cot, (((0,), (0,)), ((), ())), preferred_element_type=jnp.float32
    )
    weight_part = lax.psum_scatter(
        product * grad_scale, ("dp", "rows"), scatter_dimension=0, tiled=True
    )
    grad_weight = lax.all_gather(weight_part, "rows", axis=0, tiled=True)
    cot_pad = with_halo(cotangent, (("rows", 1),), 1)
    cot_pad = jnp.pad(cot_pad, ((0, 0), (0, 0), (1, 1), (0, 0)))
    back_grad = jnp.zeros((cell_count, channels), jnp.float32)
    tap_index = 0
    for shift_row in (-1, 0, 1):
        for shift_col in (-1, 0, 1):
            shifted = cot_pad[
                :, 1 - shift_row : 1 - shift_row + rows_here, 1 - shift_col : 1 - shift_col + width
            ].reshape(cell_count, out_channels)
            tap_weight = full_weight[tap_index * channels : (tap_index + 1) * channels]
            back_grad = back_grad + lax.dot_general(
                shifted, tap_weight, (((1,), (1,)), ((), ())), preferred_element_type=jnp.float32
            )
            tap_index = tap_index + 1
    back_grad = (back_grad * grad_scale).reshape(images, rows_here, width, channels)
    sigmoid_pre = jax.nn.sigmoid(preact)
    pre_grad = back_grad * sigmoid_pre * (1.0 + preact * (1.0 - sigmoid_pre))
    gamma_term = jnp.sum(pre_grad * normed, axis=(0, 1, 2))
    beta_term = jnp.sum(pre_grad, axis=(0, 1, 2))
    grad_bias, grad_gamma, grad_beta = lax.psum((bias_term, gamma_term, beta_term), ("dp", "rows"))
    return (output, grad_weight, grad_bias, grad_gamma, grad_beta)


def solution(mesh):
    in_specs = (
        P("dp", None, "rows", None, None),
        P("dp"),
        P("dp", None),
        P(),
        P(),
        P(),
        P("dp", "rows", None, None),
    )
    out_specs = (P("dp", "rows", None, None), P("dp", None), P(), P(), P())
    return jax.shard_map(body, mesh=mesh, in_specs=in_specs, out_specs=out_specs, check_vma=False)
```

profile of v0, /device:TPU:0, one launch (start us, length us, event | category | flops | bytes accessed | tf_op | source)
XLA Modules:
  0.0 369.2 jit_solution(6593381389159258084)
XLA Ops:
  8.0 0.7 all-gather.3.cloned.1.call-update
  8.8 0.7 broadcast_compare_fusion.2
  9.5 3.9 %fusion.42 = (bf16[2,1,8,32,1024]{4,3,2,1,0:T(8,128)(2,1)S(1)}, bf16[2,1,8,32,1024]{4,3,2,1,0:T(8,128)(2,1)S(1)}, bf16[2,1,8,32,1024]{4,3,2,1,0:T(8,128)(2,1)S(1...) fusion(bf16[2,4,8,32,1024]{4,3,2,1,0:T(8,128)(2,1)} %param.7, pred[2]{0:T(512)(128)(4,1)S(1)} %get-tuple-element.46, ...), kind=kLoop, calls=%fused_computation.79 | loop fusion | flops 1572864 | bytes 9437190 | tf_op jit(solution)/shard_map/slice | solution.py:37
  13.4 0.3 convert_reduce_fusion
  13.7 0.1 reduce_sum.60
  13.8 0.1 reduce_sum.63
  13.9 0.1 reduce_sum.61
  14.0 0.1 reduce_sum.64
  14.0 8.3 %all-reduce.3 = (f32[2,32]{1,0:T(2,128)S(1)}, f32[2,32]{1,0:T(2,128)S(1)}) all-reduce(f32[2,32]{1,0:T(2,128)S(1)} %reduce_sum.64, f32[2,32]{1,0:T(2,128)S(1)} %reduce_sum.61), channel_id=1, replica_groups=mesh['dp'=8,'rows'=4] {'rows'}, use_global_device_ids=true, to_apply=%region_5.6 | all-reduce | flops 128 | bytes 1024 | tf_op jit(solution)/shard_map/psum | solution.py:43
  22.4 0.1 sub.28
  22.4 0.1 sub.29
  22.5 0.1 mul.88
  22.6 0.1 mul.89
  22.8 4.9 %multiply_convert_fusion.1 = (bf16[2,8,32,1024]{3,2,1,0:T(8,128)(2,1)S(1)}, bf16[2,8,32,1024]{3,2,1,0:T(8,128)(2,1)}) fusion(f32[1024]{0:T(1024)S(1)} %copy-done.12, f32[1024]{0:T(1024)S(1)} %copy-done.14, f32[2,1024]{1,0:T(2,128)S(1)} %mul.89, f32[2,1024]{1,0:T(2,128)S(1)} %sub.29, bf16[2,4,8,32,1024]{4,3,2,1,0:T(8,128)(2,1)} %param.7, ...), kind=kLoop, calls=%fused_computation.16 | loop fusion | flops 6815744 | bytes 6316038 | tf_op jit(solution)/shard_map/convert_element_type | solution.py:52
  27.7 0.7 fusion.44
  28.3 1.3 collective-permute-start
  29.6 1.3 collective-permute-start.1
  30.9 1.3 broadcast_in_dim.56
  32.3 1.4 broadcast_in_dim.57
  33.6 1.3 broadcast_in_dim.62
  34.9 1.3 broadcast_in_dim.63
  36.2 1.3 broadcast_in_dim.59
  37.5 1.3 broadcast_in_dim.60
  38.8 4.1 %multiply_convert_fusion = (bf16[512,1024]{1,0:T(8,128)(2,1)S(1)}, bf16[512,1024]{1,0:T(8,128)(2,1)}) fusion(f32[1024]{0:T(1024)} %param.12, f32[1024]{0:T(1024)} %param.11, f32[2,1024]{1,0:T(2,128)S(1)} %mul.89, f32[2,1024]{1,0:T(2,128)S(1)} %sub.29, bf16[2,1,8,32,1024]{4,3,2,1,0:T(8,128)(2,1)} %get-tuple-element.22, ...), kind=kLoop, calls=%fused_computation.13 | loop fusion | flops 6815744 | bytes 6317568 | tf_op jit(solution)/shard_map/convert_element_type | solution.py:52
  42.9 0.7 fusion.6
  43.6 1.2 fusion.43
  44.8 0.1 constant_dynamic-update-slice_fusion.8
  44.9 0.1 pad_maximum_fusion
  45.0 0.1 constant_dynamic-update-slice_fusion.7
  45.1 0.1 constant_dynamic-update-slice_fusion.6
  45.2 0.1 constant_dynamic-update-slice_fusion.5
  45.3 0.1 constant_dynamic-update-slice_fusion.4
  45.3 0.1 constant_dynamic-update-slice_fusion.3
  45.4 0.1 constant_dynamic-update-slice_fusion.2
  45.5 0.1 constant_dynamic-update-slice_fusion.1
  45.6 0.1 constant_dynamic-update-slice_fusion
  45.7 3.7 copy-done.11
  49.3 9.1 %convolution_multiply_fusion = f32[9216,512]{1,0:T(8,128)} fusion(bf16[512,9216]{1,0:T(8,128)(2,1)S(1)} %constant_dynamic-update-slice_fusion, bf16[512,512]{1,0:T(8,128)(2,1)S(1)} %bitcast.107), kind=kOutput, calls=%fused_computation | convolution fusion | flops 4836556800 | bytes 28835840 | tf_op jit(solution)/shard_map/dot_general | solution.py:76
  58.6 3.8 %collective-permute-start.2 = (bf16[2,1,32,512]{3,2,1,0:T(8,128)(2,1)S(1)}, bf16[2,1,32,512]{3,2,1,0:T(8,128)(2,1)S(1)}, u32[]{:S(2)}, u32[]{:S(2)}) collective-permute-start(bf16[2,1,32,512]{3,2,1,0:T(8,128)(2,1)S(1)} %get-tuple-element.41), channel_id=1, source_target_pairs={{0,1},{1,2},{2,3},{4,5},{5,6},{6,7},{8,9},{9,10},{10,11},{12,13},{... | collective-permute-start | bytes 196616 | tf_op jit(solution)/shard_map/ppermute | solution.py:20
  62.4 1.5 collective-permute-start.3
  63.9 0.1 convert_reduce_fusion.1
  64.0 0.8 slice.156
  64.8 1.9 collective-permute-done.3
  66.8 1.0 pad_maximum_fusion.2
  67.8 0.3 fusion.38
  68.1 1.8 fusion.45
  69.9 89.8 %all-gather.3.cloned.1.call-done = bf16[9216,512]{1,0:T(8,128)(2,1)} async-done(((bf16[1152,512]{1,0:T(8,128)(2,1)}), bf16[9216,512]{1,0:T(8,128)(2,1)}) %all-gather.3.cloned.1.call-update) | async-done | bytes 9437200 | tf_op jit(solution)/shard_map/all_gather | solution.py:53
  159.7 2.0 fusion.17
  161.6 132.3 %reduce-scatter.2.cloned.1.call-done = f32[288,512]{1,0:T(8,128)} async-done(((f32[9216,512]{1,0:T(8,128)}), f32[288,512]{1,0:T(8,128)}) %reduce-scatter.2.cloned.1.call-update) | async-done | bytes 589840 | tf_op jit(solution)/shard_map/reduce_scatter | solution.py:79
  294.0 2.3 fusion.23
  296.3 2.7 fusion.13
  299.0 2.0 fusion.25
  301.1 0.7 fusion.15
  301.8 0.3 copy-done.5
  302.1 0.7 fusion.19
  302.9 0.2 copy-done.4
  303.0 0.7 fusion.21
  303.8 0.7 fusion.10
  304.6 0.4 copy-done.2
  305.0 0.1 copy-done.9
  305.2 2.6 fusion.39
  307.8 39.6 %all-reduce.2 = (f32[512]{0:T(512)}, f32[1024]{0:T(1024)}, f32[1024]{0:T(1024)}) all-reduce(f32[512]{0:T(512)S(1)} %broadcast_multiply_fusion, f32[1024]{0:T(1024)S(1)} %get-tuple-element.6, f32[1024]{0:T(1024)S(1)} %get-tuple-element.5), channel_id=1, replica_groups=mesh['dp'=8,'rows'=4] {'dp','rows'}, use_global_device_ids=true, to_apply=%region_8.9 | all-reduce | flops 2560 | bytes 20480 | tf_op jit(solution)/shard_map/psum | solution.py:102
  347.4 11.1 %fusion.9 = bf16[512,512]{1,0:T(8,128)(2,1)} fusion(bf16[512,9216]{1,0:T(8,128)(2,1)} %copy-done.11, bf16[9216,512]{1,0:T(8,128)(2,1)} %all-gather.3.cloned.1.call-done, bf16[512,512]{1,0:T(8,128)(2,1)S(1)} %bitcast.125, f32[512]{0:T(512)S(1)} %copy-done.19), kind=kOutput, calls=%fused_computation.25 | convolution fusion | flops 4832886784 | bytes 19924992 | tf_op jit(solution)/shard_map/dot_general | solution.py:66
  358.5 3.3 copy.29
  (47 shorter events, 0.3 us)
Async XLA Ops:
  8.0 151.7 %all-gather.3.cloned.1.call-start = ((), (), s32[]{:S(2)}) async-start(), calls=%async_computation.1 | async-start | bytes 10616832 | tf_op jit(solution)/shard_map/all_gather | solution.py:53
  8.7 285.2 %reduce-scatter.2.cloned.1.call-start = ((), (), s32[]{:S(2)}) async-start(), calls=%async_computation.2 | async-start | bytes 19464192 | tf_op jit(solution)/shard_map/reduce_scatter | solution.py:79
  9.4 13.3 %copy-start.16 = (pred[2]{0:T(512)(128)(4,1)}, pred[2]{0:T(512)(128)(4,1)S(1)}, u32[]{:S(2)}) copy-start(pred[2]{0:T(512)(128)(4,1)S(1)} %get-tuple-element.47) | copy-start | bytes 10
  9.4 13.3 %copy-start.17 = (pred[2]{0:T(512)(128)(4,1)}, pred[2]{0:T(512)(128)(4,1)S(1)}, u32[]{:S(2)}) copy-start(pred[2]{0:T(512)(128)(4,1)S(1)} %get-tuple-element.46) | copy-start | bytes 10
  9.4 13.3 %copy-start.18 = (pred[2]{0:T(512)(128)(4,1)}, pred[2]{0:T(512)(128)(4,1)S(1)}, u32[]{:S(2)}) copy-start(pred[2]{0:T(512)(128)(4,1)S(1)} %get-tuple-element.45) | copy-start | bytes 10
  9.5 13.3 %copy-start.12 = (f32[1024]{0:T(1024)S(1)}, f32[1024]{0:T(1024)}, u32[]{:S(2)}) copy-start(f32[1024]{0:T(1024)} %param.12) | copy-start | bytes 12292
  9.5 13.3 %copy-start.14 = (f32[1024]{0:T(1024)S(1)}, f32[1024]{0:T(1024)}, u32[]{:S(2)}) copy-start(f32[1024]{0:T(1024)} %param.11) | copy-start | bytes 12292
  28.3 14.6 %collective-permute-start = (bf16[2,1,32,1024]{3,2,1,0:T(8,128)(2,1)}, bf16[2,1,32,1024]{3,2,1,0:T(8,128)(2,1)S(1)}, u32[]{:S(2)}, u32[]{:S(2)}) collective-permute-start(bf16[2,1,32,1024]{3,2,1,0:T(8,128)(2,1)} %get-tuple-element.31), channel_id=1, source_target_pairs={{0,1},{1,2},{2,3},{4,5},{5,6},{6,7},{8,9},{9,10},{10,11},{12,13},{... | collective-permute-start | bytes 393224 | tf_op jit(solution)/shard_map/ppermute | solution.py:20
  29.6 13.3 %collective-permute-start.1 = (bf16[2,1,32,1024]{3,2,1,0:T(8,128)(2,1)S(1)}, bf16[2,1,32,1024]{3,2,1,0:T(8,128)(2,1)S(1)}, u32[]{:S(2)}, u32[]{:S(2)}) collective-permute-start(bf16[2,1,32,1024]{3,2,1,0:T(8,128)(2,1)S(1)} %get-tuple-element.32), channel_id=1, source_target_pairs={{1,0},{2,1},{3,2},{5,4},{6,5},{7,6},{9,8},{10,9},{11,10},{13,12},{... | collective-permute-start | bytes 393224 | tf_op jit(solution)/shard_map/ppermute | solution.py:22
  45.5 3.8 %copy-start = (bf16[2,8,32,512]{3,2,1,0:T(8,128)(2,1)S(1)}, bf16[2,8,32,512]{3,2,1,0:T(8,128)(2,1)}, u32[]{:S(2)}) copy-start(bf16[2,8,32,512]{3,2,1,0:T(8,128)(2,1)} %param.13) | copy-start | bytes 1572868
  45.7 3.7 copy-start.11
  58.5 5.5 %copy-start.3 = (bf16[2,8,32,1024]{3,2,1,0:T(8,128)(2,1)S(1)}, bf16[2,8,32,1024]{3,2,1,0:T(8,128)(2,1)}, u32[]{:S(2)}) copy-start(bf16[2,8,32,1024]{3,2,1,0:T(8,128)(2,1)} %get-tuple-element.17) | copy-start | bytes 3145732
  58.5 300.0 %all-gather.5.cloned.1.call-start = ((), (), s32[]{:S(2)}) async-start(), calls=%async_computation.3 | async-start | bytes 2949120 | tf_op jit(solution)/shard_map/all_gather | solution.py:82
  58.6 6.3 %collective-permute-start.2 = (bf16[2,1,32,512]{3,2,1,0:T(8,128)(2,1)S(1)}, bf16[2,1,32,512]{3,2,1,0:T(8,128)(2,1)S(1)}, u32[]{:S(2)}, u32[]{:S(2)}) collective-permute-start(bf16[2,1,32,512]{3,2,1,0:T(8,128)(2,1)S(1)} %get-tuple-element.41), channel_id=1, source_target_pairs={{0,1},{1,2},{2,3},{4,5},{5,6},{6,7},{8,9},{9,10},{10,11},{12,13},{... | collective-permute-start | bytes 196616 | tf_op jit(solution)/shard_map/ppermute | solution.py:20
  62.4 4.4 %collective-permute-start.3 = (bf16[2,1,32,512]{3,2,1,0:T(8,128)(2,1)S(1)}, bf16[2,1,32,512]{3,2,1,0:T(8,128)(2,1)S(1)}, u32[]{:S(2)}, u32[]{:S(2)}) collective-permute-start(bf16[2,1,32,512]{3,2,1,0:T(8,128)(2,1)S(1)} %get-tuple-element.42), channel_id=1, source_target_pairs={{1,0},{2,1},{3,2},{5,4},{6,5},{7,6},{9,8},{10,9},{11,10},{13,12},{... | collective-permute-start | bytes 196616 | tf_op jit(solution)/shard_map/ppermute | solution.py:22
  293.9 2.3 copy-start.8
  294.0 5.0 %copy-start.7 = (bf16[2,8,32,512]{3,2,1,0:T(8,128)(2,1)S(1)}, bf16[2,8,32,512]{3,2,1,0:T(8,128)(2,1)}, u32[]{:S(2)}) copy-start(bf16[2,8,32,512]{3,2,1,0:T(8,128)(2,1)} %get-tuple-element.33) | copy-start | bytes 1572868
  294.0 7.1 %copy-start.1 = (bf16[9216,512]{1,0:T(8,128)(2,1)S(1)}, bf16[9216,512]{1,0:T(8,128)(2,1)}, u32[]{:S(2)}) copy-start(bf16[9216,512]{1,0:T(8,128)(2,1)} %all-gather.3.cloned.1.call-done) | copy-start | bytes 28311556
  299.0 2.1 copy-start.6
  301.0 1.1 copy-start.5
  301.8 1.2 copy-start.4
  303.8 1.2 copy-start.2
  303.8 1.3 copy-start.9
  303.8 1.3 copy-start.13
  303.8 1.3 copy-start.15
  305.2 42.3 %copy-start.10 = (bf16[2,8,32,512]{3,2,1,0:T(8,128)(2,1)S(1)}, bf16[2,8,32,512]{3,2,1,0:T(8,128)(2,1)}, u32[]{:S(2)}) copy-start(bf16[2,8,32,512]{3,2,1,0:T(8,128)(2,1)} %slice.156) | copy-start | bytes 1572868
  305.2 42.3 %copy-start.19 = (f32[512]{0:T(512)S(1)}, f32[512]{0:T(512)}, u32[]{:S(2)}) copy-start(f32[512]{0:T(512)} %param.10) | copy-start | bytes 6148
Sparse Core Ops, SparseCore 0:
  11.0 148.6 all-gather.2
Sparse Core Ops, SparseCore 1:
  58.6 235.3 reduce-scatter.1
  295.4 23.5 all-gather.4
where the time goes:
time: 370 us; the launch traced here: 369 us
  waiting for transfers between devices  225 us (61%)
  blocking collectives  47.9 us (13%)
  matrix products  34.7 us (9%)
  local copies, waits for them, and re-layouts  21.5 us (6%)
  other arithmetic  16.3 us (4%)
  between operations  15.9 us (4%)
  starting transfers between devices  7.99 us (2%)
    reduce_scatter x1, waiting for transfers between devices, body(): lax.psum_scatter(product * grad_scale, ('dp', 'rows'), scatter_dimension=...  132 us
    all_gather x1, waiting for transfers between devices, body(): full_weight = lax.all_gather(conv_weight, 'dp', axis=0, tiled=True)  89.8 us
    psum x1, blocking collectives, body(): lax.psum((bias_term, gamma_term, beta_term), ('dp', 'rows'))  39.6 us
    dot_general x9, matrix products, body(): lax.dot_general(shifted, tap_weight, (((1,), (1,)), ((), ())), preferred_...  14.5 us
    dot_general x1, matrix products, body(): jnp.dot(patches, full_weight, preferred_element_type=jnp.float32)  11.1 us
    dot_general x1, matrix products, body(): lax.dot_general(patches, flat_cot, (((0,), (0,)), ((), ())), preferred_el...  9.13 us
    convert_element_type x2, other arithmetic, body(): activated = jax.nn.silu(preact).astype(jnp.bfloat16)  9.01 us
    unnamed x49, local copies, waits for them, and re-layouts  8.64 us
  transfers between devices with their start and end apart: 7, of which 3 were waited for; matrix products, arithmetic and copies ran while one was open for 17% of the time, Pallas kernels for 0%

commit v1 on v0

v1 whole, which is shorter than its diff:
```python
import functools
import math

import jax
import jax.numpy as jnp
from jax import lax
from jax.experimental import pallas as pl
from jax.experimental.pallas import tpu as pltpu
from jax.sharding import PartitionSpec as P

GROUPS = 32


EPSILON = 1e-05


CONV_DIMS = ("NHWC", "HWIO", "NHWC")


CHUNKS = 3


VMEM_BYTES = 48 * 1024 * 1024


MESH = pl.DeviceIdType.MESH


def greet(owners, split):
    dp, rows = lax.axis_index("dp"), lax.axis_index("rows")
    lane, side = dp // 2, dp % 2
    peers = [{"rows": lax.rem(rows + k, split)} for k in range(1, split)]
    peers += [{"dp": lax.rem(dp + k, owners)} for k in range(1, owners)]
    barrier = pltpu.get_barrier_semaphore()
    for peer in peers:
        pl.semaphore_signal(barrier, inc=1, device_id=peer, device_id_type=MESH)
    pl.semaphore_wait(barrier, len(peers))


def remote(src, dst, sems, at, peer):
    return pltpu.make_async_remote_copy(
        src_ref=src, dst_ref=dst, send_sem=sems.at[0, at], recv_sem=sems.at[1, at],
        device_id=peer, device_id_type=MESH,
    )


def gather_start(axis, count, src, dst, far, near):
    me = lax.axis_index(axis)
    lane, side, lanes = me // 2, me % 2, count // 2
    far_copies = []
    for k in range(1, lanes):
        copy = remote(src, dst.at[me], far, k, {axis: lax.rem(lane + k, lanes) * 2 + side})
        copy.start()
        far_copies.append(copy)
    near_copies = [remote(src, dst.at[me], near, 0, {axis: lane * 2 + 1 - side})]
    near_copies[0].start()
    return far_copies, near_copies


def gather_relay(axis, count, dst, far_copies, near_copies, near):
    me = lax.axis_index(axis)
    lane, side, lanes = me // 2, me % 2, count // 2
    for k in range(1, lanes):
        far_copies[k - 1].wait_recv()
        slot = lax.rem(lane - k + lanes, lanes) * 2 + side
        copy = remote(dst.at[slot], dst.at[slot], near, k, {axis: lane * 2 + 1 - side})
        copy.start()
        near_copies.append(copy)


def gather_end(far_copies, near_copies):
    for copy in far_copies:
        copy.wait_send()
    for copy in near_copies:
        copy.wait()


def spread_kernel(owners, split, weight, picked, cot, all_weight, all_picked, all_cot,
                  wfar, wnear, cfar, cnear, psems, lsems):
    dp, rows = lax.axis_index("dp"), lax.axis_index("rows")
    greet(owners, split)
    wcopies = gather_start("dp", owners, weight, all_weight, wfar, wnear)
    direct = []
    for k in range(1, split):
        to = lax.rem(rows + k, split)
        copy = remote(picked.at[to], all_picked.at[rows], psems, k, {"rows": to})
        copy.start()
        direct.append(copy)
    ccopies = gather_start("rows", split, cot, all_cot, cfar, cnear)
    own = [
        pltpu.make_async_copy(weight, all_weight.at[dp], lsems.at[0]),
        pltpu.make_async_copy(picked.at[rows], all_picked.at[rows], lsems.at[1]),
        pltpu.make_async_copy(cot, all_cot.at[rows], lsems.at[2]),
    ]
    for copy in own:
        copy.start()
    gather_relay("dp", owners, all_weight, *wcopies, wnear)
    gather_relay("rows", split, all_cot, *ccopies, cnear)
    for copy in own + direct:
        copy.wait()
    gather_end(*ccopies)
    gather_end(*wcopies)


def spread(owners, split, weight, picked, cot):
    dma = lambda n: pltpu.SemaphoreType.DMA((2, n))
    return pl.pallas_call(
        functools.partial(spread_kernel, owners, split),
        out_shape=(
            jax.ShapeDtypeStruct((owners,) + weight.shape, weight.dtype),
            jax.ShapeDtypeStruct(picked.shape, picked.dtype),
            jax.ShapeDtypeStruct((split,) + cot.shape, cot.dtype),
        ),
        in_specs=[pl.BlockSpec(memory_space=pl.ANY)] * 3,
        out_specs=[pl.BlockSpec(memory_space=pl.ANY)] * 3,
        scratch_shapes=[
            dma(owners // 2), dma(owners // 2), dma(split // 2), dma(split // 2), dma(split),
            pltpu.SemaphoreType.DMA((3,)),
        ],
        compiler_params=pltpu.CompilerParams(collective_id=1, has_side_effects=True),
        name="spread",
    )(weight, picked, cot)


def combine_kernel(owners, split, sent, conv, small, weight_out, conv_out, small_out,
                   ybuf, zsend, zbuf, sbuf, tbuf, ysems, zsems, csems, ssems, tsems, *gsems):
    dp, rows = lax.axis_index("dp"), lax.axis_index("rows")
    lane, side, lanes = dp // 2, dp % 2, owners // 2
    pair = {"dp": lane * 2 + 1 - side}
    greet(owners, split)
    ycopies = {}
    for c in range(CHUNKS):
        for k in [*range(1, lanes), 0]:
            to = lax.rem(lane + k, lanes)
            copy = remote(sent.at[to * 2 + 1 - side, c], ybuf.at[k, c], ysems, k * CHUNKS + c, pair)
            copy.start()
            ycopies[k, c] = copy
    scopies = []
    sbuf[rows] = small[...]
    for k in range(1, split):
        copy = remote(small, sbuf.at[rows], ssems, k, {"rows": lax.rem(rows + k, split)})
        copy.start()
        scopies.append(copy)
    ccopies = []
    for k in range(1, split):
        to = lax.rem(rows + k, split)
        copy = remote(conv.at[to], conv_out.at[rows], csems, k, {"rows": to})
        copy.start()
        ccopies.append(copy)
    conv_out[rows] = conv[rows]
    zcopies = {}
    tcopies = []
    gathers = []
    for c in range(CHUNKS):
        for k in range(1, lanes):
            to = lax.rem(lane + k, lanes)
            ycopies[k, c].wait_recv()
            zsend[k, c] = (
                sent[to * 2 + side, c].astype(jnp.float32) + ybuf[k, c].astype(jnp.float32)
            ).astype(jnp.bfloat16)
            at = k * CHUNKS + c
            copy = remote(zsend.at[k, c], zbuf.at[k, c], zsems, at, {"dp": to * 2 + side})
            copy.start()
            zcopies[k, c] = copy
        ycopies[0, c].wait_recv()
        if c == 0:
            for copy in scopies:
                copy.wait()
            tbuf[dp] = functools.reduce(jnp.add, [sbuf[i] for i in range(split)])
            for k in range(1, owners):
                copy = remote(tbuf.at[dp], tbuf.at[dp], tsems, k, {"dp": lax.rem(dp + k, owners)})
                copy.start()
                tcopies.append(copy)
    for c in range(CHUNKS):
        total = sent[lane * 2 + side, c].astype(jnp.float32) + ybuf[0, c].astype(jnp.float32)
        for k in range(1, lanes):
            zcopies[k, c].wait_recv()
            total = total + zbuf[k, c].astype(jnp.float32)
        weight_out[c, rows] = total
        dst = weight_out.at[c]
        gathers.append(
            gather_start("rows", split, dst.at[rows], dst, gsems[2 * c], gsems[2 * c + 1])
        )
    for c in range(CHUNKS):
        gather_relay("rows", split, weight_out.at[c], *gathers[c], gsems[2 * c + 1])
    for copy in tcopies + ccopies:
        copy.wait()
    small_out[...] = functools.reduce(jnp.add, [tbuf[i] for i in range(owners)])
    for copy in [*ycopies.values(), *zcopies.values()]:
        copy.wait_send()
    for pieces in gathers:
        gather_end(*pieces)


def combine(owners, split, sent, conv, small):
    lanes = owners // 2
    block = sent.shape[1:]
    dma = lambda n: pltpu.SemaphoreType.DMA((2, n))
    vmem = pl.BlockSpec(memory_space=pltpu.VMEM)
    return pl.pallas_call(
        functools.partial(combine_kernel, owners, split),
        out_shape=(
            jax.ShapeDtypeStruct((CHUNKS, split) + block[1:], jnp.float32),
            jax.ShapeDtypeStruct(conv.shape, conv.dtype),
            jax.ShapeDtypeStruct(small.shape, small.dtype),
        ),
        in_specs=[vmem] * 3,
        out_specs=[vmem] * 3,
        scratch_shapes=[
            pltpu.VMEM((lanes,) + block, jnp.bfloat16),
            pltpu.VMEM((lanes,) + block, jnp.bfloat16),
            pltpu.VMEM((lanes,) + block, jnp.bfloat16),
            pltpu.VMEM((split,) + small.shape, jnp.float32),
            pltpu.VMEM((owners,) + small.shape, jnp.float32),
            dma(lanes * CHUNKS), dma(lanes * CHUNKS), dma(split), dma(split), dma(owners),
        ] + [dma(split // 2)] * (2 * CHUNKS),
        compiler_params=pltpu.CompilerParams(
            collective_id=2, has_side_effects=True, vmem_limit_bytes=VMEM_BYTES
        ),
        name="combine",
    )(sent, conv, small)


def body(candidates, winners, conv_weight, conv_bias, gamma, beta, cotangent):
    images, cand_count, rows_here, width, channels = candidates.shape
    own_rows, out_channels = conv_weight.shape
    split = lax.axis_size("rows")
    owners = lax.axis_size("dp")
    me = lax.axis_index("rows")
    size = channels // GROUPS
    rows_all = rows_here * split
    share = channels // split
    taps = own_rows * owners // channels
    grain = size if own_rows % (split * size) == 0 else math.gcd(own_rows // split, size // split)
    runs = share // grain
    groups_here = GROUPS // split if grain == size else GROUPS
    size_here = share // groups_here
    own_runs = own_rows // (split * grain)
    own_share = own_rows // split
    lined = out_channels if own_share % (16 * CHUNKS) == 0 else 128
    grad_scale = float(images * owners * rows_all * width) ** (-0.5)

    def take(vector):
        return lax.dynamic_index_in_dim(
            vector.reshape(runs, split, grain), me, 1, keepdims=False
        ).reshape(share)

    mine = lax.dynamic_index_in_dim(
        conv_weight.reshape(own_runs, split, grain, out_channels), me, 1, keepdims=False
    ).reshape(-1, lined)

    picked = candidates[:, 0]
    for cand_index in range(1, cand_count):
        picked = jnp.where(
            (winners == cand_index)[:, None, None, None], candidates[:, cand_index], picked
        )
    place = jnp.arange(share)
    flat_picked = picked.reshape(-1, channels)
    sorted_picked = jnp.stack(
        [
            jnp.dot(
                flat_picked,
                (
                    jnp.arange(channels)[:, None]
                    == (place // grain * split + part) * grain + place % grain
                ).astype(jnp.bfloat16),
                preferred_element_type=jnp.float32,
            ).astype(jnp.bfloat16)
            for part in range(split)
        ]
    )
    weight, local, cot = spread(
        owners, split, mine, sorted_picked, cotangent.reshape(-1, out_channels)
    )
    weight = weight.reshape(3, 3, share, out_channels)
    local = local.reshape(split, images, rows_here, width, share)
    local = jnp.swapaxes(local, 0, 1).reshape(images, rows_all, width, share)
    cot = cot.reshape(split, images, rows_here, width, out_channels)
    cot = jnp.swapaxes(cot, 0, 1).reshape(images, rows_all, width, out_channels)

    wide = local.astype(jnp.float32)
    count = rows_all * width * size
    sums = jnp.sum(wide, axis=(1, 2)).reshape(images, groups_here, size_here).sum(axis=2)
    squares = jnp.sum(wide * wide, axis=(1, 2)).reshape(images, groups_here, size_here).sum(axis=2)
    if grain < size:
        sums, squares = lax.psum((sums, squares), "rows")
    mean = sums / count
    inverse = lax.rsqrt(squares / count - mean * mean + EPSILON)
    mean = jnp.repeat(mean, size_here, axis=1)[:, None, None, :]
    inverse = jnp.repeat(inverse, size_here, axis=1)[:, None, None, :]
    normed = (wide - mean) * inverse
    preact = normed * take(gamma) + take(beta)
    sigmoid_pre = jax.nn.sigmoid(preact)
    activated = (preact * sigmoid_pre).astype(jnp.bfloat16)

    padded = jnp.pad(activated, ((0, 0), (1, 1), (1, 1), (0, 0)))
    patches = jnp.concatenate(
        [
            padded[:, a : a + rows_all, b : b + width].reshape(-1, share)
            for a in range(3)
            for b in range(3)
        ],
        axis=1,
    )
    product = lax.dot_general(
        patches, cot.reshape(-1, out_channels), (((0,), (0,)), ((), ())),
        preferred_element_type=jnp.float32,
    )
    sent = (product * grad_scale).astype(jnp.bfloat16).reshape(owners, CHUNKS, -1, lined)

    conv_part = jnp.dot(
        patches, weight.reshape(-1, out_channels), preferred_element_type=jnp.float32
    ).astype(jnp.bfloat16).reshape(images, split, -1, out_channels)
    conv_part = jnp.swapaxes(conv_part, 0, 1)

    flipped = jnp.swapaxes(jnp.flip(weight, (0, 1)), 2, 3)
    back_grad = grad_scale * lax.conv_general_dilated(
        cot, flipped, (1, 1), ((1, 1), (1, 1)),
        dimension_numbers=CONV_DIMS, preferred_element_type=jnp.float32,
    )
    pre_grad = back_grad * sigmoid_pre * (1.0 + preact * (1.0 - sigmoid_pre))
    gamma_term = jnp.sum(pre_grad * normed, axis=(0, 1, 2)).reshape(runs, 1, grain)
    beta_term = jnp.sum(pre_grad, axis=(0, 1, 2)).reshape(runs, 1, grain)
    here = (jnp.arange(split) == me).reshape(1, split, 1)
    gamma_term = jnp.where(here, gamma_term, 0.0).reshape(channels)
    beta_term = jnp.where(here, beta_term, 0.0).reshape(channels)
    bias_term = jnp.sum(cotangent.astype(jnp.float32), axis=(0, 1, 2)) * grad_scale
    small = jnp.concatenate([gamma_term, beta_term, bias_term]).reshape(-1, 128)

    weight_sum, conv_got, small_sum = combine(owners, split, sent, conv_part, small)
    weight_sum = jnp.swapaxes(weight_sum, 0, 1).reshape(split, own_runs, grain, out_channels)
    grad_weight = jnp.swapaxes(weight_sum, 0, 1).reshape(own_rows, out_channels)
    conv_sum = jnp.sum(conv_got.astype(jnp.float32), axis=0).reshape(
        images, rows_here, width, out_channels
    )
    output = (
        conv_sum + conv_bias + picked[..., :out_channels].astype(jnp.float32)
    ).astype(jnp.bfloat16)
    small_sum = small_sum.reshape(-1)
    grad_gamma, grad_beta, grad_bias = (
        small_sum[:channels], small_sum[channels : 2 * channels], small_sum[2 * channels :]
    )
    return (output, grad_weight, grad_bias, grad_gamma, grad_beta)


def solution(mesh):
    in_specs = (
        P("dp", None, "rows", None, None),
        P("dp"),
        P("dp", None),
        P(),
        P(),
        P(),
        P("dp", "rows", None, None),
    )
    out_specs = (P("dp", "rows", None, None), P("dp", None), P(), P(), P())
    return jax.shard_map(body, mesh=mesh, in_specs=in_specs, out_specs=out_specs, check_vma=False)
```

time: 370 us -> 158 us (0.43)
  waiting for transfers between devices: 225 us -> 0 us
  Pallas kernels: 0 us -> 92.5 us
  blocking collectives: 47.9 us -> 0 us
  between operations: 15.9 us -> 0.98 us
  starting transfers between devices: 7.99 us -> 0 us
  matrix products: 34.7 us -> 28.5 us
  other arithmetic: 16.3 us -> 10.3 us
    reduce_scatter x1 -> x0, waiting for transfers between devices: 132 us -> none  [body(): lax.psum_scatter(product * grad_scale, ('dp', 'rows'), scatter_dimension=...]
    pallas_call x0 -> x2, Pallas kernels: none -> 92.5 us  [the longest x1 51.4 us: combine(): pl.pallas_call(functools.partial(combine_kernel, owners, split), out_shap...]
    all_gather x2 -> x0, waiting for transfers between devices: 89.8 us -> none  [the longest x1 89.8 us: body(): full_weight = lax.all_gather(conv_weight, 'dp', axis=0, tiled=True)]
    psum x2 -> x0, blocking collectives: 47.9 us -> none  [the longest x1 39.6 us: body(): lax.psum((bias_term, gamma_term, beta_term), ('dp', 'rows'))]
    dot_general x11 -> x6, matrix products: 34.7 us -> 13.6 us  [the longest x1 6.35 us: body(): lax.dot_general(patches, cot.reshape(-1, out_channels), (((0,), (0,)), ((...]
    conv_general_dilated x0 -> x1, matrix products: none -> 14.9 us  [body(): lax.conv_general_dilated(cot, flipped, (1, 1), ((1, 1), (1, 1)), dimensio...]
    ppermute x4 -> x0, starting transfers between devices: 7.87 us -> none  [the longest x2 5.11 us: with_halo(): lax.ppermute(tail, axis, [(i, (i + 1) % count) for i in range(ends)])]
    broadcast_in_dim x6, local copies, waits for them, and re-layouts: 7.85 us -> 0.49 us  [body(): jnp.where((winners == cand_index)[:, None, None, None], candidates[:, can...]
  transfers between devices with their start and end apart: 7 -> 0, of which waited for: 3 -> 0; matrix products, arithmetic and copies ran while one was open for 17% -> 0% of each run, Pallas kernels for 0% -> 0%
where the time goes in v1:
time: 158 us; the launch traced here: 157 us
  Pallas kernels  92.5 us (59%)
  matrix products  28.5 us (18%)
  local copies, waits for them, and re-layouts  24.5 us (16%)
  other arithmetic  10.3 us (7%)
    pallas_call x1, Pallas kernels, combine(): pl.pallas_call(functools.partial(combine_kernel, owners, split), out_shap...  51.4 us
    pallas_call x1, Pallas kernels, spread(): pl.pallas_call(functools.partial(spread_kernel, owners, split), out_shape...  41.1 us
    conv_general_dilated x1, matrix products, body(): lax.conv_general_dilated(cot, flipped, (1, 1), ((1, 1), (1, 1)), dimensio...  14.9 us
    unnamed x33, local copies, waits for them, and re-layouts  6.88 us
    dot_general x1, matrix products, body(): lax.dot_general(patches, cot.reshape(-1, out_channels), (((0,), (0,)), ((...  6.35 us
    dot_general x1, matrix products, body(): jnp.dot(patches, weight.reshape(-1, out_channels), preferred_element_type...  5.2 us
    squeeze x1, local copies, waits for them, and re-layouts, body(): candidates[:, cand_index]  4.59 us
    slice x1, local copies, waits for them, and re-layouts, body(): padded[:, a:a + rows_all, b:b + width].reshape(-1, share)  3.96 us

profile of v1, /device:TPU:0, one launch (start us, length us, event | category | flops | bytes accessed | tf_op | source)
XLA Modules:
  0.0 156.8 jit_solution(2964422132818368403)
XLA Ops:
  0.7 1.2 copy-done
  1.9 0.7 broadcast_compare_fusion.2
  2.6 0.1 broadcast_in_dim.87
  2.6 0.1 broadcast_in_dim.88
  2.7 0.1 broadcast_in_dim.93
  2.8 0.1 broadcast_in_dim.94
  2.9 0.1 broadcast_in_dim.90
  3.0 0.1 broadcast_in_dim.91
  3.1 1.2 convert_reduce_fusion.1
  4.3 0.8 reshape.183
  5.0 0.8 reshape.184
  5.8 0.1 add.160
  5.9 0.1 mul.134
  6.0 0.7 constant_dynamic-slice_fusion
  6.7 4.6 %slice_bitcast_fusion.4 = (bf16[2,8,32,1024]{3,2,1,0:T(8,128)(2,1)}, bf16[2,8,32,1024]{3,2,1,0:T(8,128)(2,1)}, bf16[2,8,32,1024]{3,2,1,0:T(8,128)(2,1)}, bf16[2,...) fusion(bf16[2,4,8,32,1024]{4,3,2,1,0:T(8,128)(2,1)} %param.7), kind=kLoop, calls=%fused_computation.93 | loop fusion | bytes 12582912 | tf_op jit(solution)/shard_map/squeeze | solution.py:255
  11.3 0.6 fusion.14
  12.0 0.5 fusion.12
  12.5 0.5 fusion.11
  13.0 0.5 fusion.10
  13.5 0.5 fusion.9
  14.0 1.1 pad_maximum_fusion.picked
  15.1 41.1 %spread.1 = (bf16[8,288,512]{2,1,0:T(8,128)(2,1)}, bf16[4,512,256]{2,1,0:T(8,128)(2,1)}, bf16[4,512,512]{2,1,0:T(8,128)(2,1)}) custom-call(bf16[288,512]{1,0:T(8,128)(2,1)} %bitcast.141, bf16[4,512,256]{2,1,0:T(8,128)(2,1)} %pad_maximum_fusion.picked, bf16[512,512]{1,0:T(8,128)(2,1)} %bitcast.136), custom_call_target="tpu_custom_call" | custom-call | tf_op jit(solution)/shard_map/spread/pallas_call | solution.py:107
  56.2 1.9 %copy.90 = bf16[4,2,8,32,512]{4,3,2,0,1:T(8,128)(2,1)S(1)} copy(bf16[4,2,8,32,512]{4,3,2,1,0:T(8,128)(2,1)} %bitcast.139) | data formatting | bytes 4194304 | tf_op jit(solution)/shard_map/reshape | solution.py:278
  58.1 0.3 copy.89
  58.4 2.1 %copy-done.11 = bf16[8,288,512]{2,1,0:T(8,128)(2,1)S(1)} copy-done((bf16[8,288,512]{2,1,0:T(8,128)(2,1)S(1)}, bf16[8,288,512]{2,1,0:T(8,128)(2,1)}, u32[]{:S(2)}) %copy-start.11) | copy-done | bytes 2359320
  60.5 14.9 %fusion.7 = f32[2,32,32,256]{3,0,2,1:T(2,128)} fusion(bf16[3,3,256,512]{3,2,1,0:T(8,128)(2,1)S(1)} %bitcast.142, bf16[2,32,32,512]{3,2,1,0:T(8,128)(2,1)S(1)} %bitcast.137), kind=kOutput, calls=%fused_computation.21 | convolution fusion | flops 4632608768 | bytes 6553600 | tf_op jit(solution)/shard_map/conv_general_dilated | solution.py:317
  75.4 0.3 bitcast_convert_fusion
  75.7 0.3 bitcast_reduce_fusion
  76.0 0.1 reshape.181
  76.0 0.1 reduce_sum.73
  76.1 0.1 reshape.182
  76.2 0.1 reduce_sum.75
  76.3 0.1 broadcast_in_dim.96
  76.4 0.1 sub.40
  76.5 0.1 mul.131
  76.6 2.7 %fusion.6 = (f32[2,32,32,256]{3,2,1,0:T(8,128)S(1)}, bf16[2,32,32,256]{3,2,1,0:T(8,128)(2,1)S(1)}) fusion(f32[2,32,32,256]{3,0,2,1:T(2,128)} %fusion.7, f32[2,32,32,256]{3,2,1,0:T(8,128)S(1)} %bitcast.120, f32[256]{0:T(256)S(1)} %add.160, f32[256]{0:T(256)S(1)} %mul.134, f32[2,256]{1,0:T(2,128)S(1)} %mul.131, f32[2,256]{1,0:T(2,128)S(1)} %sub.40), kind=kLoop, calls=%fused_computation.13 | loop fusion | flops 7864320 | bytes 7346176 | tf_op jit(solution)/shard_map/mul | solution.py:321
  79.3 0.6 multiply_reduce_fusion
  79.9 0.1 broadcast_in_dim.99
  80.0 0.1 broadcast_in_dim.102
  80.1 0.1 broadcast_select_fusion.1
  80.1 0.1 select_n.107
  80.2 0.1 select_n.109
  80.3 4.0 %pad_slice_fusion = (bf16[2,32,32,256]{3,2,1,0:T(8,128)(2,1)S(1)}, bf16[2,32,32,256]{3,2,1,0:T(8,128)(2,1)S(1)}, bf16[2,32,32,256]{3,2,1,0:T(8,128)(2,1)S(1)}, b...) fusion(bf16[2,32,32,256]{3,2,1,0:T(8,128)(2,1)S(1)} %get-tuple-, ...), kind=kLoop, calls=%fused_computation.23 | loop fusion | bytes 9437184 | tf_op jit(solution)/shard_map/slice | solution.py:299
  84.4 0.1 constant_dynamic-update-slice_fusion.7
  84.4 0.1 constant_dynamic-update-slice_fusion.6
  84.5 0.1 constant_dynamic-update-slice_fusion.5
  84.6 0.7 constant_dynamic-update-slice_fusion.4
  85.3 0.1 constant_dynamic-update-slice_fusion.3
  85.3 0.1 constant_dynamic-update-slice_fusion.2
  85.4 0.1 constant_dynamic-update-slice_fusion.1
  85.6 1.5 copy-done.12
  87.1 5.2 %convolution_convert_fusion = bf16[2048,512]{1,0:T(8,128)(2,1)S(1)} fusion(bf16[2048,2304]{1,0:T(8,128)(2,1)S(1)} %constant_dynamic-update-slice_fusion, bf16[2304,512]{1,0:T(8,128)(2,1)S(1)} %bitcast.143), kind=kOutput, calls=%fused_computation.3 | convolution fusion | flops 4832886784 | bytes 13893632 | tf_op jit(solution)/shard_map/dot_general | solution.py:311
  92.3 6.4 %fusion = bf16[2304,512]{1,0:T(8,128)(2,1)} fusion(bf16[2048,2304]{1,0:T(8,128)(2,1)S(1)} %constant_dynamic-update-slice_fusion, bf16[2048,512]{1,0:T(8,128)(2,1)S(1)} %bitcast.138), kind=kOutput, calls=%fused_computation.1 | convolution fusion | flops 4834197504 | bytes 13893632 | tf_op jit(solution)/shard_map/dot_general | solution.py:305
  98.7 0.1 copy.111
  98.8 51.4 %combine.1 = (f32[3,4,96,512]{3,2,1,0:T(8,128)}, bf16[4,2,256,512]{3,2,1,0:T(8,128)(2,1)S(1)}, f32[20,128]{1,0:T(8,128)S(1)}) custom-call(bf16[8,3,96,512]{3,2,1,0:T(8,128)(2,1)} %bitcast.133, bf16[4,2,256,512]{3,2,1,0:T(8,128)(2,1)S(1)} %bitcast.119, f32[20,128]{1,0:T(8,128)S(1)} %maximum_bitcast_fusion.small), custom_call_target="tpu_custom_call" | custom-call | tf_op jit(solution)/shard_map/combine/pallas_call | solution.py:200
  150.3 0.3 convert_reduce_fusion
  150.7 0.8 copy-done.3
  151.5 0.3 copy-done.4
  151.8 0.3 copy-done.5
  152.1 1.6 %add_convert_fusion = bf16[2,8,32,512]{3,2,1,0:T(8,128)(2,1)} fusion(f32[2,8,32,512]{3,2,1,0:T(8,128)S(1)} %bitcast.132, bf16[2,8,32,1024]{3,2,1,0:T(8,128)(2,1)S(1)} %copy-done.4, bf16[2,8,32,1024]{3,2,1,0:T(8,128)(2,1)S(1)} %copy-done.5, bf16[2,8,32,1024]{3,2,1,0:T(8,128)(2,1)S(1)} %copy-done.6, bf16[2,8,32,1024]{3,2,1,0:T(8,128)(2,1)S(1)} %copy-done.3, ...), kind=kLoop, calls=%fused_computation.43 | loop fusion | flops 1835008 | bytes 3672070 | tf_op jit(solution)/shard_map/convert_element_type | solution.py:338
  153.8 0.2 copy.94
  154.0 1.6 %copy.95 = f32[9,4,32,512]{3,2,1,0:T(8,128)} copy(f32[9,4,32,512]{3,2,0,1:T(8,128)S(1)} %bitcast.122) | data formatting | bytes 4718592 | tf_op jit(solution)/shard_map/transpose | solution.py:332
  155.6 0.6 slice_bitcast_fusion.2
  156.2 0.6 slice_bitcast_fusion
  (30 shorter events, 0.3 us)
Async XLA Ops:
  0.6 1.3 copy-start
  56.2 2.0 %copy-start.2 = (bf16[4,512,256]{2,1,0:T(8,128)(2,1)S(1)}, bf16[4,512,256]{2,1,0:T(8,128)(2,1)}, u32[]{:S(2)}) copy-start(bf16[4,512,256]{2,1,0:T(8,128)(2,1)} %get-tuple-element.11) | copy-start | bytes 3145732
  58.1 17.3 %copy-start.8 = (bf16[4,2,8,32,512]{4,3,2,0,1:T(8,128)(2,1)}, bf16[4,2,8,32,512]{4,3,2,0,1:T(8,128)(2,1)S(1)}, u32[]{:S(2)}) copy-start(bf16[4,2,8,32,512]{4,3,2,0,1:T(8,128)(2,1)S(1)} %copy.90) | copy-start | bytes 6291460
  58.1 2.4 %copy-start.11 = (bf16[8,288,512]{2,1,0:T(8,128)(2,1)S(1)}, bf16[8,288,512]{2,1,0:T(8,128)(2,1)}, u32[]{:S(2)}) copy-start(bf16[8,288,512]{2,1,0:T(8,128)(2,1)} %get-tuple-element.13) | copy-start | bytes 7077892
  85.4 1.7 %copy-start.12 = (bf16[8,288,512]{2,1,0:T(8,128)(2,1)S(1)}, bf16[8,288,512]{2,1,0:T(8,128)(2,1)}, u32[]{:S(2)}) copy-start(bf16[8,288,512]{2,1,0:T(8,128)(2,1)} %get-tuple-element.13) | copy-start | bytes 7077892
  87.1 5.2 %copy-start.9 = (bf16[4,2,8,32,512]{4,3,2,0,1:T(8,128)(2,1)S(1)}, bf16[4,2,8,32,512]{4,3,2,0,1:T(8,128)(2,1)}, u32[]{:S(2)}) copy-start(bf16[4,2,8,32,512]{4,3,2,0,1:T(8,128)(2,1)} %copy-done.8) | copy-start | bytes 6291460
  98.8 51.9 %copy-start.6 = (bf16[2,8,32,1024]{3,2,1,0:T(8,128)(2,1)S(1)}, bf16[2,8,32,1024]{3,2,1,0:T(8,128)(2,1)}, u32[]{:S(2)}) copy-start(bf16[2,8,32,1024]{3,2,1,0:T(8,128)(2,1)} %get-tuple-element.24) | copy-start | bytes 3145732
  150.2 1.2 copy-start.3
  150.3 1.5 copy-start.4
  150.3 1.8 %copy-start.5 = (bf16[2,8,32,1024]{3,2,1,0:T(8,128)(2,1)S(1)}, bf16[2,8,32,1024]{3,2,1,0:T(8,128)(2,1)}, u32[]{:S(2)}) copy-start(bf16[2,8,32,1024]{3,2,1,0:T(8,128)(2,1)} %get-tuple-element.23) | copy-start | bytes 3145732
  150.3 1.8 %copy-start.10 = (f32[512]{0:T(512)S(1)}, f32[512]{0:T(512)}, u32[]{:S(2)}) copy-start(f32[512]{0:T(512)} %param.10) | copy-start | bytes 6148
  150.6 3.1 %copy-start.7 = (f32[3,4,96,512]{3,2,1,0:T(8,128)S(1)}, f32[3,4,96,512]{3,2,1,0:T(8,128)}, u32[]{:S(2)}) copy-start(f32[3,4,96,512]{3,2,1,0:T(8,128)} %get-tuple-element.15) | copy-start | bytes 7077892
  154.0 2.8 %copy-start.1 = (bf16[1152,512]{1,0:T(8,128)(2,1)S(1)}, bf16[1152,512]{1,0:T(8,128)(2,1)}, u32[]{:S(2)}) copy-start(bf16[1152,512]{1,0:T(8,128)(2,1)} %param.9) | copy-start | bytes 3538948

commit v2 on v1

--- a/solution.py
+++ b/solution.py
@@ -75,11 +75,27 @@
         copy.wait()
 
 
+class Part:
+    def __init__(self, ref, chunk):
+        self.ref, self.chunk = ref, chunk
+
+    @property
+    def at(self):
+        return self
+
+    def __getitem__(self, slot):
+        return self.ref.at[slot, self.chunk]
+
+
 def spread_kernel(owners, split, weight, picked, cot, all_weight, all_picked, all_cot,
-                  wfar, wnear, cfar, cnear, psems, lsems):
+                  cfar, cnear, psems, lsems, *wsems):
     dp, rows = lax.axis_index("dp"), lax.axis_index("rows")
     greet(owners, split)
-    wcopies = gather_start("dp", owners, weight, all_weight, wfar, wnear)
+    parts = [Part(all_weight, c) for c in range(CHUNKS)]
+    wcopies = [
+        gather_start("dp", owners, weight.at[c], parts[c], wsems[2 * c], wsems[2 * c + 1])
+        for c in range(CHUNKS)
+    ]
     direct = []
     for k in range(1, split):
         to = lax.rem(rows + k, split)
@@ -94,12 +110,15 @@
     ]
     for copy in own:
         copy.start()
-    gather_relay("dp", owners, all_weight, *wcopies, wnear)
-    gather_relay("rows", split, all_cot, *ccopies, cnear)
+    for c in range(CHUNKS):
+        gather_relay("dp", owners, parts[c], *wcopies[c], wsems[2 * c + 1])
+        if c == CHUNKS // 2:
+            gather_relay("rows", split, all_cot, *ccopies, cnear)
     for copy in own + direct:
         copy.wait()
     gather_end(*ccopies)
-    gather_end(*wcopies)
+    for pieces in wcopies:
+        gather_end(*pieces)
 
 
 def spread(owners, split, weight, picked, cot):
@@ -114,9 +133,8 @@
         in_specs=[pl.BlockSpec(memory_space=pl.ANY)] * 3,
         out_specs=[pl.BlockSpec(memory_space=pl.ANY)] * 3,
         scratch_shapes=[
-            dma(owners // 2), dma(owners // 2), dma(split // 2), dma(split // 2), dma(split),
-            pltpu.SemaphoreType.DMA((3,)),
-        ],
+            dma(split // 2), dma(split // 2), dma(split), pltpu.SemaphoreType.DMA((3,)),
+        ] + [dma(owners // 2)] * (2 * CHUNKS),
         compiler_params=pltpu.CompilerParams(collective_id=1, has_side_effects=True),
         name="spread",
     )(weight, picked, cot)
@@ -247,7 +265,7 @@
 
     mine = lax.dynamic_index_in_dim(
         conv_weight.reshape(own_runs, split, grain, out_channels), me, 1, keepdims=False
-    ).reshape(-1, lined)
+    ).reshape(CHUNKS, -1, lined)
 
     picked = candidates[:, 0]
     for cand_index in range(1, cand_count):

time: 158 us -> 151 us (0.956)
  Pallas kernels: 92.5 us -> 86.1 us
    pallas_call x1, Pallas kernels: 51.4 us -> 45.6 us  [combine(): pl.pallas_call(functools.partial(combine_kernel, owners, split), out_shap...]
where the time goes in v2:
time: 151 us; the launch traced here: 150 us
  Pallas kernels  86.1 us (57%)
  matrix products  28.5 us (19%)
  local copies, waits for them, and re-layouts  24.5 us (16%)
  other arithmetic  10.3 us (7%)
    pallas_call x1, Pallas kernels, combine(): pl.pallas_call(functools.partial(combine_kernel, owners, split), out_shap...  45.6 us
    pallas_call x1, Pallas kernels, spread(): pl.pallas_call(functools.partial(spread_kernel, owners, split), out_shape...  40.5 us
    conv_general_dilated x1, matrix products, body(): lax.conv_general_dilated(cot, flipped, (1, 1), ((1, 1), (1, 1)), dimensio...  14.9 us
    unnamed x33, local copies, waits for them, and re-layouts  6.88 us
    dot_general x1, matrix products, body(): lax.dot_general(patches, cot.reshape(-1, out_channels), (((0,), (0,)), ((...  6.35 us
    dot_general x1, matrix products, body(): jnp.dot(patches, weight.reshape(-1, out_channels), preferred_element_type...  5.2 us
    squeeze x1, local copies, waits for them, and re-layouts, body(): candidates[:, cand_index]  4.59 us
    slice x1, local copies, waits for them, and re-layouts, body(): padded[:, a:a + rows_all, b:b + width].reshape(-1, share)  3.96 us

profile of v2, /device:TPU:0, one launch (start us, length us, event | category | flops | bytes accessed | tf_op | source)
XLA Modules:
  0.0 150.4 jit_solution(7293454025406772608)
XLA Ops:
  0.7 1.2 copy-done
  1.9 0.7 broadcast_compare_fusion.2
  2.6 0.1 broadcast_in_dim.87
  2.6 0.1 broadcast_in_dim.88
  2.7 0.1 broadcast_in_dim.93
  2.8 0.1 broadcast_in_dim.94
  2.9 0.1 broadcast_in_dim.90
  3.0 0.1 broadcast_in_dim.91
  3.1 1.2 convert_reduce_fusion.1
  4.3 0.8 reshape.183
  5.0 0.8 reshape.184
  5.8 0.1 add.160
  5.9 0.1 mul.134
  6.0 0.7 constant_dynamic-slice_fusion
  6.7 4.6 %slice_bitcast_fusion.4 = (bf16[2,8,32,1024]{3,2,1,0:T(8,128)(2,1)}, bf16[2,8,32,1024]{3,2,1,0:T(8,128)(2,1)}, bf16[2,8,32,1024]{3,2,1,0:T(8,128)(2,1)}, bf16[2,...) fusion(bf16[2,4,8,32,1024]{4,3,2,1,0:T(8,128)(2,1)} %param.7), kind=kLoop, calls=%fused_computation.93 | loop fusion | bytes 12582912 | tf_op jit(solution)/shard_map/squeeze | solution.py:273
  11.3 0.6 fusion.14
  12.0 0.5 fusion.12
  12.5 0.5 fusion.11
  13.0 0.5 fusion.10
  13.5 0.5 fusion.9
  14.0 1.1 pad_maximum_fusion.picked
  15.1 40.5 %spread.1 = (bf16[8,3,96,512]{3,2,1,0:T(8,128)(2,1)}, bf16[4,512,256]{2,1,0:T(8,128)(2,1)}, bf16[4,512,512]{2,1,0:T(8,128)(2,1)}) custom-call(bf16[3,96,512]{2,1,0:T(8,128)(2,1)} %bitcast.141, bf16[4,512,256]{2,1,0:T(8,128)(2,1)} %pad_maximum_fusion.picked, bf16[512,512]{1,0:T(8,128)(2,1)} %bitcast.136), custom_call_target="tpu_custom_call" | custom-call | tf_op jit(solution)/shard_map/spread/pallas_call | solution.py:126
  55.7 1.9 %copy.90 = bf16[4,2,8,32,512]{4,3,2,0,1:T(8,128)(2,1)S(1)} copy(bf16[4,2,8,32,512]{4,3,2,1,0:T(8,128)(2,1)} %bitcast.139) | data formatting | bytes 4194304 | tf_op jit(solution)/shard_map/reshape | solution.py:296
  57.6 0.3 copy.89
  57.9 2.1 %copy-done.11 = bf16[8,3,96,512]{3,2,1,0:T(8,128)(2,1)S(1)} copy-done((bf16[8,3,96,512]{3,2,1,0:T(8,128)(2,1)S(1)}, bf16[8,3,96,512]{3,2,1,0:T(8,128)(2,1)}, u32[]{:S(2)}) %copy-start.11) | copy-done | bytes 2359320
  60.0 14.9 %fusion.7 = f32[2,32,32,256]{3,0,2,1:T(2,128)} fusion(bf16[3,3,256,512]{3,2,1,0:T(8,128)(2,1)S(1)} %bitcast.142, bf16[2,32,32,512]{3,2,1,0:T(8,128)(2,1)S(1)} %bitcast.137), kind=kOutput, calls=%fused_computation.21 | convolution fusion | flops 4632608768 | bytes 6553600 | tf_op jit(solution)/shard_map/conv_general_dilated | solution.py:335
  74.9 0.3 bitcast_convert_fusion
  75.2 0.3 bitcast_reduce_fusion
  75.4 0.1 reshape.181
  75.5 0.1 reduce_sum.73
  75.6 0.1 reshape.182
  75.7 0.1 reduce_sum.75
  75.8 0.1 broadcast_in_dim.96
  75.9 0.1 sub.40
  76.0 0.1 mul.131
  76.1 2.7 %fusion.6 = (f32[2,32,32,256]{3,2,1,0:T(8,128)S(1)}, bf16[2,32,32,256]{3,2,1,0:T(8,128)(2,1)S(1)}) fusion(f32[2,32,32,256]{3,0,2,1:T(2,128)} %fusion.7, f32[2,32,32,256]{3,2,1,0:T(8,128)S(1)} %bitcast.120, f32[256]{0:T(256)S(1)} %add.160, f32[256]{0:T(256)S(1)} %mul.134, f32[2,256]{1,0:T(2,128)S(1)} %mul.131, f32[2,256]{1,0:T(2,128)S(1)} %sub.40), kind=kLoop, calls=%fused_computation.13 | loop fusion | flops 7864320 | bytes 7346176 | tf_op jit(solution)/shard_map/mul | solution.py:339
  78.8 0.6 multiply_reduce_fusion
  79.4 0.1 broadcast_in_dim.99
  79.5 0.1 broadcast_in_dim.102
  79.5 0.1 broadcast_select_fusion.1
  79.6 0.1 select_n.107
  79.7 0.1 select_n.109
  79.8 4.0 %pad_slice_fusion = (bf16[2,32,32,256]{3,2,1,0:T(8,128)(2,1)S(1)}, bf16[2,32,32,256]{3,2,1,0:T(8,128)(2,1)S(1)}, bf16[2,32,32,256]{3,2,1,0:T(8,128)(2,1)S(1)}, b...) fusion(bf16[2,32,32,256]{3,2,1,0:T(8,128)(2,1)S(1)} %get-tuple-, ...), kind=kLoop, calls=%fused_computation.23 | loop fusion | bytes 9437184 | tf_op jit(solution)/shard_map/slice | solution.py:317
  83.8 0.1 constant_dynamic-update-slice_fusion.7
  83.9 0.1 constant_dynamic-update-slice_fusion.6
  84.0 0.1 constant_dynamic-update-slice_fusion.5
  84.1 0.7 constant_dynamic-update-slice_fusion.4
  84.7 0.1 constant_dynamic-update-slice_fusion.3
  84.8 0.1 constant_dynamic-update-slice_fusion.2
  84.9 0.1 constant_dynamic-update-slice_fusion.1
  85.1 1.5 copy-done.12
  86.6 5.2 %convolution_convert_fusion = bf16[2048,512]{1,0:T(8,128)(2,1)S(1)} fusion(bf16[2048,2304]{1,0:T(8,128)(2,1)S(1)} %constant_dynamic-update-slice_fusion, bf16[2304,512]{1,0:T(8,128)(2,1)S(1)} %bitcast.143), kind=kOutput, calls=%fused_computation.3 | convolution fusion | flops 4832886784 | bytes 13893632 | tf_op jit(solution)/shard_map/dot_general | solution.py:329
  91.8 6.4 %fusion = bf16[2304,512]{1,0:T(8,128)(2,1)} fusion(bf16[2048,2304]{1,0:T(8,128)(2,1)S(1)} %constant_dynamic-update-slice_fusion, bf16[2048,512]{1,0:T(8,128)(2,1)S(1)} %bitcast.138), kind=kOutput, calls=%fused_computation.1 | convolution fusion | flops 4834197504 | bytes 13893632 | tf_op jit(solution)/shard_map/dot_general | solution.py:323
  98.1 0.1 copy.111
  98.3 45.6 %combine.1 = (f32[3,4,96,512]{3,2,1,0:T(8,128)}, bf16[4,2,256,512]{3,2,1,0:T(8,128)(2,1)S(1)}, f32[20,128]{1,0:T(8,128)S(1)}) custom-call(bf16[8,3,96,512]{3,2,1,0:T(8,128)(2,1)} %bitcast.133, bf16[4,2,256,512]{3,2,1,0:T(8,128)(2,1)S(1)} %bitcast.119, f32[20,128]{1,0:T(8,128)S(1)} %maximum_bitcast_fusion.small), custom_call_target="tpu_custom_call" | custom-call | tf_op jit(solution)/shard_map/combine/pallas_call | solution.py:218
  143.9 0.3 convert_reduce_fusion
  144.3 0.8 copy-done.3
  145.1 0.3 copy-done.4
  145.4 0.3 copy-done.5
  145.7 1.6 %add_convert_fusion = bf16[2,8,32,512]{3,2,1,0:T(8,128)(2,1)} fusion(f32[2,8,32,512]{3,2,1,0:T(8,128)S(1)} %bitcast.132, bf16[2,8,32,1024]{3,2,1,0:T(8,128)(2,1)S(1)} %copy-done.4, bf16[2,8,32,1024]{3,2,1,0:T(8,128)(2,1)S(1)} %copy-done.5, bf16[2,8,32,1024]{3,2,1,0:T(8,128)(2,1)S(1)} %copy-done.6, bf16[2,8,32,1024]{3,2,1,0:T(8,128)(2,1)S(1)} %copy-done.3, ...), kind=kLoop, calls=%fused_computation.43 | loop fusion | flops 1835008 | bytes 3672070 | tf_op jit(solution)/shard_map/convert_element_type | solution.py:356
  147.4 0.2 copy.94
  147.6 1.6 %copy.95 = f32[9,4,32,512]{3,2,1,0:T(8,128)} copy(f32[9,4,32,512]{3,2,0,1:T(8,128)S(1)} %bitcast.122) | data formatting | bytes 4718592 | tf_op jit(solution)/shard_map/transpose | solution.py:350
  149.2 0.6 slice_bitcast_fusion.2
  149.8 0.6 slice_bitcast_fusion
  (30 shorter events, 0.3 us)
Async XLA Ops:
  0.6 1.3 copy-start
  55.7 2.0 %copy-start.2 = (bf16[4,512,256]{2,1,0:T(8,128)(2,1)S(1)}, bf16[4,512,256]{2,1,0:T(8,128)(2,1)}, u32[]{:S(2)}) copy-start(bf16[4,512,256]{2,1,0:T(8,128)(2,1)} %get-tuple-element.11) | copy-start | bytes 3145732
  57.6 17.3 %copy-start.8 = (bf16[4,2,8,32,512]{4,3,2,0,1:T(8,128)(2,1)}, bf16[4,2,8,32,512]{4,3,2,0,1:T(8,128)(2,1)S(1)}, u32[]{:S(2)}) copy-start(bf16[4,2,8,32,512]{4,3,2,0,1:T(8,128)(2,1)S(1)} %copy.90) | copy-start | bytes 6291460
  57.6 2.4 %copy-start.11 = (bf16[8,3,96,512]{3,2,1,0:T(8,128)(2,1)S(1)}, bf16[8,3,96,512]{3,2,1,0:T(8,128)(2,1)}, u32[]{:S(2)}) copy-start(bf16[8,3,96,512]{3,2,1,0:T(8,128)(2,1)} %get-tuple-element.13) | copy-start | bytes 7077892
  84.9 1.7 %copy-start.12 = (bf16[8,3,96,512]{3,2,1,0:T(8,128)(2,1)S(1)}, bf16[8,3,96,512]{3,2,1,0:T(8,128)(2,1)}, u32[]{:S(2)}) copy-start(bf16[8,3,96,512]{3,2,1,0:T(8,128)(2,1)} %get-tuple-element.13) | copy-start | bytes 7077892
  86.6 5.2 %copy-start.9 = (bf16[4,2,8,32,512]{4,3,2,0,1:T(8,128)(2,1)S(1)}, bf16[4,2,8,32,512]{4,3,2,0,1:T(8,128)(2,1)}, u32[]{:S(2)}) copy-start(bf16[4,2,8,32,512]{4,3,2,0,1:T(8,128)(2,1)} %copy-done.8) | copy-start | bytes 6291460
  98.3 46.0 %copy-start.6 = (bf16[2,8,32,1024]{3,2,1,0:T(8,128)(2,1)S(1)}, bf16[2,8,32,1024]{3,2,1,0:T(8,128)(2,1)}, u32[]{:S(2)}) copy-start(bf16[2,8,32,1024]{3,2,1,0:T(8,128)(2,1)} %get-tuple-element.24) | copy-start | bytes 3145732
  143.9 1.2 copy-start.3
  143.9 1.5 %copy-start.4 = (bf16[2,8,32,1024]{3,2,1,0:T(8,128)(2,1)S(1)}, bf16[2,8,32,1024]{3,2,1,0:T(8,128)(2,1)}, u32[]{:S(2)}) copy-start(bf16[2,8,32,1024]{3,2,1,0:T(8,128)(2,1)} %get-tuple-element.22) | copy-start | bytes 3145732
  143.9 1.8 %copy-start.5 = (bf16[2,8,32,1024]{3,2,1,0:T(8,128)(2,1)S(1)}, bf16[2,8,32,1024]{3,2,1,0:T(8,128)(2,1)}, u32[]{:S(2)}) copy-start(bf16[2,8,32,1024]{3,2,1,0:T(8,128)(2,1)} %get-tuple-element.23) | copy-start | bytes 3145732
  143.9 1.8 %copy-start.10 = (f32[512]{0:T(512)S(1)}, f32[512]{0:T(512)}, u32[]{:S(2)}) copy-start(f32[512]{0:T(512)} %param.10) | copy-start | bytes 6148
  144.3 3.1 %copy-start.7 = (f32[3,4,96,512]{3,2,1,0:T(8,128)S(1)}, f32[3,4,96,512]{3,2,1,0:T(8,128)}, u32[]{:S(2)}) copy-start(f32[3,4,96,512]{3,2,1,0:T(8,128)} %get-tuple-element.15) | copy-start | bytes 7077892
  147.6 2.8 %copy-start.1 = (bf16[1152,512]{1,0:T(8,128)(2,1)S(1)}, bf16[1152,512]{1,0:T(8,128)(2,1)}, u32[]{:S(2)}) copy-start(bf16[1152,512]{1,0:T(8,128)(2,1)} %param.9) | copy-start | bytes 3538948
